TPU v7x, 32 devices: a whole 2x2x4 slice. The times are simulated.
32 devices in a mesh: dp: 8 (over z, core), mp: 4 (over y, x).
Axes of the slice: x: 2, y: 2, z: 4, core: 2. Of those that a mesh axis runs over, the one named last changes fastest.
Arguments:
- tokens: bfloat16 [37632, 512], P(('dp', 'mp')), may hold values from -6 to 6
- cotangent: bfloat16 [37632, 512], P(('dp', 'mp')), may hold values from -6 to 6
- w_in: float32 [512, 2, 1536], P(None, None, 'mp'), may hold values from -0.31819805 to 0.31819805
- w_out: float32 [1536, 512], P('mp'), may hold values from -0.15625 to 0.15625
- spatial: float32 [196, 196], replicated, may hold values from -0.4375 to 0.4375
- model_vectors: float32 [3, 512], replicated, may hold values from 0.1 to 1.9
- gate_vectors: float32 [4, 1536], P(None, 'mp'), may hold values from 0.1 to 1.9
- patch_bias: float32 [196], replicated, may hold values from -3 to 3
- moment_in: float32 [512, 2, 1536], P(None, None, 'mp'), may hold values from -448 to 448
- moment_out: float32 [1536, 512], P('mp'), may hold values from -640 to 640
- moment_mix: float32 [196, 196], replicated, may hold values from -1024 to 1024
- first_model: float32 [3, 512], replicated, may hold values from -112 to 112
- second_model: float32 [3, 512], replicated, may hold values from 1881.6 to 7526.4
- first_gate: float32 [4, 1536], P(None, 'mp'), may hold values from -48 to 48
- second_gate: float32 [4, 1536], P(None, 'mp'), may hold values from 301.056 to 1204.224
- first_patch: float32 [196], replicated, may hold values from -112 to 112
- second_patch: float32 [196], replicated, may hold values from 1769.472 to 7372.8
Outputs:
- output: bfloat16 [37632, 512], P(('dp', 'mp'))
- grad_tokens: bfloat16 [37632, 512], P(('dp', 'mp'))
- grad_w_in: float32 [512, 2, 1536], P(None, None, 'mp')
- grad_w_out: float32 [1536, 512], P('mp')
- grad_spatial: float32 [196, 196], replicated
- grad_model: float32 [3, 512], replicated
- grad_gate: float32 [4, 1536], P(None, 'mp')
- grad_patch: float32 [196], replicated
- new_moment_in: float32 [512, 2, 1536], P(None, None, 'mp')
- new_moment_out: float32 [1536, 512], P('mp')
- new_moment_mix: float32 [196, 196], replicated
- new_second_model: float32 [3, 512], replicated
- new_second_gate: float32 [4, 1536], P(None, 'mp')
- new_second_patch: float32 [196], replicated
- new_w_in: float32 [512, 2, 1536], P(None, None, 'mp')
- new_w_out: float32 [1536, 512], P('mp')
- new_spatial: float32 [196, 196], replicated
- new_model: float32 [3, 512], replicated
- new_gate: float32 [4, 1536], P(None, 'mp')
- new_patch: float32 [196], replicated
All inputs are finite; a program needn't handle non-finite values.
Results may differ from a plain program's by a relative error of at most 0.0096.
The roundings to bfloat16 on the way count: a program that leaves them out, or rounds other values in their place, can miss the bound.
Values may be sent and summed in bfloat16 or wider, within the bound.
No kernel may reach another device: no remote copies, remote signals or barrier semaphores. Data moves between devices by JAX's collectives and lax.ppermute only.
A program may use at most 256 MiB of HBM per device.

v0:
```python
import math

import jax
import jax.numpy as jnp
from jax import lax
from jax.sharding import PartitionSpec as P

STEP = 10


EPSILON = 1e-05
HIGHEST = lax.Precision.HIGHEST
COEF_FIRST = 3.4445
COEF_SECOND = -4.775
COEF_THIRD = 2.0315
MOMENTUM = 0.95
MUON_RATE = 0.2
ADAM_RATE = 0.3
DECAY_RATE = 0.01
BETA_FIRST = 0.9
BETA_SECOND = 0.95


def row_norm(rows, gain, shift):
    row_mean = jnp.mean(rows, axis=-1, keepdims=True)
    centred = rows - row_mean
    inv_std = lax.rsqrt(jnp.mean(centred * centred, axis=-1, keepdims=True) + EPSILON)
    unit_rows = centred * inv_std
    return (unit_rows * gain + shift, unit_rows, inv_std)


def newton_step(ortho, gram):
    polynomial = COEF_SECOND * gram + COEF_THIRD * jnp.dot(gram, gram, precision=HIGHEST)
    return COEF_FIRST * ortho + jnp.dot(polynomial, ortho, precision=HIGHEST)


def orthogonal(moment):
    ortho = moment / (jnp.sqrt(jnp.sum(moment * moment)) + 1e-07)
    for sweep in range(5):
        ortho = newton_step(ortho, jnp.dot(ortho, ortho.T, precision=HIGHEST))
    return ortho


def adam_update(param_now, grad_now, first_old, second_old):
    first_new = BETA_FIRST * first_old + (1.0 - BETA_FIRST) * grad_now
    second_new = BETA_SECOND * second_old + (1.0 - BETA_SECOND) * grad_now * grad_now
    first_hat = first_new / (1.0 - BETA_FIRST**STEP)
    second_hat = second_new / (1.0 - BETA_SECOND**STEP)
    updated = param_now * (1.0 - ADAM_RATE * DECAY_RATE) - ADAM_RATE * first_hat / (
        jnp.sqrt(second_hat) + 1e-08
    )
    return (second_new, updated)


def per_device(
    tokens,
    cotangent,
    w_in,
    w_out,
    spatial,
    model_vectors,
    gate_vectors,
    patch_bias,
    moment_in,
    moment_out,
    moment_mix,
    first_model,
    second_model,
    first_gate,
    second_gate,
    first_patch,
    second_patch,
):
    model_width = tokens.shape[1]
    shard_width = w_in.shape[2]
    full_gate = shard_width * lax.axis_size("mp")
    patches = spatial.shape[0]
    rows_in = tokens.astype(jnp.float32)
    normed_full, unit_in, inv_in = row_norm(rows_in, model_vectors[0], model_vectors[1])
    normed = normed_full.astype(jnp.bfloat16)
    gathered = lax.all_gather(normed, "mp", axis=0, tiled=True)
    weight_cat = w_in.astype(jnp.bfloat16).reshape(model_width, 2 * shard_width)
    hidden = jnp.dot(gathered, weight_cat, preferred_element_type=jnp.float32) + gate_vectors[
        0:2
    ].reshape(2 * shard_width)
    activated, gelu_pull = jax.vjp(jax.nn.gelu, hidden)
    value_half = activated[:, :shard_width]
    gate_half = activated[:, shard_width:]
    gate_sums = lax.psum((jnp.sum(gate_half, axis=1), jnp.sum(gate_half * gate_half, axis=1)), "mp")
    gate_mean = gate_sums[0] / full_gate
    gate_var = gate_sums[1] / full_gate - gate_mean * gate_mean
    inv_gate = lax.rsqrt(gate_var + EPSILON)[:, None]
    gate_unit = (gate_half - gate_mean[:, None]) * inv_gate
    gate_normed = (gate_unit * gate_vectors[2] + gate_vectors[3]).astype(jnp.bfloat16)
    spatial_low = spatial.astype(jnp.bfloat16)
    images = gate_normed.reshape(-1, patches, shard_width)
    mixed_rows = (
        jnp.einsum("pq,bqc->bpc", spatial_low, images, preferred_element_type=jnp.float32)
        + patch_bias[None, :, None]
    )
    mixed_rows = mixed_rows.reshape(-1, shard_width)
    gated_vals = (value_half * mixed_rows).astype(jnp.bfloat16)
    w_out_low = w_out.astype(jnp.bfloat16)
    block_rows = gated_vals
    branch = lax.psum_scatter(
        jnp.dot(block_rows, w_out_low, preferred_element_type=jnp.float32),
        "mp",
        scatter_dimension=0,
        tiled=True,
    )
    output = (rows_in + branch + model_vectors[2]).astype(jnp.bfloat16)
    cot_all = lax.all_gather(cotangent, "mp", axis=0, tiled=True)
    grad_w_out = jnp.einsum("tc,td->cd", gated_vals, cot_all, preferred_element_type=jnp.float32)
    grad_gated = jnp.einsum("td,cd->tc", cot_all, w_out_low, preferred_element_type=jnp.float32)
    grad_value = grad_gated * mixed_rows
    grad_mixed = (grad_gated * value_half).astype(jnp.bfloat16)
    grad_images = grad_mixed.reshape(-1, patches, shard_width)
    grad_spatial = jnp.einsum(
        "bpc,bqc->pq", grad_images, images, preferred_element_type=jnp.float32
    )
    grad_patch = jnp.sum(grad_images, axis=(0, 2), dtype=jnp.float32)
    grad_gate_normed = jnp.einsum(
        "pq,bpc->bqc", spatial_low, grad_images, preferred_element_type=jnp.float32
    ).reshape(-1, shard_width)
    grad_gate_gain = jnp.sum(grad_gate_normed * gate_unit, axis=0)
    grad_gate_shift = jnp.sum(grad_gate_normed, axis=0)
    grad_unit = grad_gate_normed * gate_vectors[2]
    back_sums = lax.psum((jnp.sum(grad_unit, axis=1), jnp.sum(grad_unit * gate_unit, axis=1)), "mp")
    grad_gate_half = inv_gate * (
        grad_unit
        - back_sums[0][:, None] / full_gate
        - gate_unit * (back_sums[1][:, None] / full_gate)
    )
    grad_activated = jnp.concatenate([grad_value, grad_gate_half], axis=1)
    grad_hidden = gelu_pull(grad_activated)[0].astype(jnp.bfloat16)
    grad_bias_in = jnp.sum(grad_hidden, axis=0, dtype=jnp.float32).reshape(2, shard_width)
    grad_w_in = jnp.einsum(
        "td,tc->dc", gathered, grad_hidden, preferred_element_type=jnp.float32
    ).reshape(model_width, 2, shard_width)
    block_rows = grad_hidden
    grad_normed = lax.psum_scatter(
        jnp.einsum("tc,dc->td", block_rows, weight_cat, preferred_element_type=jnp.float32),
        "mp",
        scatter_dimension=0,
        tiled=True,
    )
    grad_unit_in = grad_normed * model_vectors[0]
    grad_tokens = cotangent.astype(jnp.float32) + inv_in * (
        grad_unit_in
        - jnp.mean(grad_unit_in, axis=1, keepdims=True)
        - unit_in * jnp.mean(grad_unit_in * unit_in, axis=1, keepdims=True)
    )
    model_part = jnp.stack(
        [
            jnp.sum(grad_normed * unit_in, axis=0),
            jnp.sum(grad_normed, axis=0),
            jnp.sum(cotangent, axis=0, dtype=jnp.float32),
        ]
    )
    gate_part = jnp.concatenate(
        [grad_bias_in, jnp.stack([grad_gate_gain, grad_gate_shift])], axis=0
    )
    grad_w_in, grad_w_out, grad_gate = lax.psum((grad_w_in, grad_w_out, gate_part), "dp")
    grad_spatial, grad_patch, grad_model = lax.psum(
        (grad_spatial, grad_patch, model_part), ("dp", "mp")
    )
    new_moment_in = MOMENTUM * moment_in + grad_w_in
    new_moment_out = MOMENTUM * moment_out + grad_w_out
    new_moment_mix = MOMENTUM * moment_mix + grad_spatial
    flat_in = new_moment_in.reshape(model_width, 2 * shard_width)
    flat_out = new_moment_out.T
    norm_sums = lax.psum((jnp.sum(flat_in * flat_in), jnp.sum(flat_out * flat_out)), "mp")
    ortho_in = flat_in / (jnp.sqrt(norm_sums[0]) + 1e-07)
    ortho_out = flat_out / (jnp.sqrt(norm_sums[1]) + 1e-07)
    for sweep in range(5):
        gram_sums = lax.psum(
            (
                jnp.dot(ortho_in, ortho_in.T, precision=HIGHEST),
                jnp.dot(ortho_out, ortho_out.T, precision=HIGHEST),
            ),
            "mp",
        )
        ortho_in = newton_step(ortho_in, gram_sums[0])
        ortho_out = newton_step(ortho_out, gram_sums[1])
    shrink_by = 1.0 - MUON_RATE * DECAY_RATE
    new_w_in = w_in * shrink_by - MUON_RATE * 0.2 * math.sqrt(
        max(model_width, 2 * full_gate)
    ) * ortho_in.reshape(model_width, 2, shard_width)
    new_w_out = (
        w_out * shrink_by - MUON_RATE * 0.2 * math.sqrt(max(model_width, full_gate)) * ortho_out.T
    )
    new_spatial = spatial * shrink_by - MUON_RATE * 0.2 * math.sqrt(patches) * orthogonal(
        new_moment_mix
    )
    new_second_model, new_model = adam_update(model_vectors, grad_model, first_model, second_model)
    new_second_gate, new_gate = adam_update(gate_vectors, grad_gate, first_gate, second_gate)
    new_second_patch, new_patch = adam_update(patch_bias, grad_patch, first_patch, second_patch)
    return (
        output,
        grad_tokens.astype(jnp.bfloat16),
        grad_w_in,
        grad_w_out,
        grad_spatial,
        grad_model,
        grad_gate,
        grad_patch,
        new_moment_in,
        new_moment_out,
        new_moment_mix,
        new_second_model,
        new_second_gate,
        new_second_patch,
        new_w_in,
        new_w_out,
        new_spatial,
        new_model,
        new_gate,
        new_patch,
    )


def solution(mesh):
    return jax.shard_map(
        per_device,
        mesh=mesh,
        in_specs=(
            P(("dp", "mp"), None),
            P(("dp", "mp"), None),
            P(None, None, "mp"),
            P("mp", None),
            P(),
            P(),
            P(None, "mp"),
            P(),
            P(None, None, "mp"),
            P("mp", None),
            P(),
            P(),
            P(),
            P(None, "mp"),
            P(None, "mp"),
            P(),
            P(),
        ),
        out_specs=(
            P(("dp", "mp"), None),
            P(("dp", "mp"), None),
            P(None, None, "mp"),
            P("mp", None),
            P(),
            P(),
            P(None, "mp"),
            P(),
            P(None, None, "mp"),
            P("mp", None),
            P(),
            P(),
            P(None, "mp"),
            P(),
            P(None, None, "mp"),
            P("mp", None),
            P(),
            P(),
            P(None, "mp"),
            P(),
        ),
        check_vma=False,
    )
```

profile of v0, /device:TPU:0, one launch (start us, length us, event | category | flops | bytes accessed | tf_op | source)
XLA Modules:
  0.0 1164.9 jit_solution(5468534132290305281)
XLA Ops:
  17.1 59.2 %all-gather.3.cloned.1.call-done = bf16[4704,512]{1,0:T(8,128)(2,1)} async-done(((bf16[1176,512]{1,0:T(8,128)(2,1)}), bf16[4704,512]{1,0:T(8,128)(2,1)}) %all-gather.3.cloned.1.call-update) | async-done | bytes 4816912 | tf_op jit(solution)/shard_map/all_gather | solution.py:81
  76.3 16.5 %multiply_multiply_fusion.2 = (f32[4704,768]{1,0:T(8,128)}, f32[4704,768]{1,0:T(8,128)}) fusion(f32[768]{0:T(1024)S(1)} %add.291, bf16[4704,512]{1,0:T(8,128)(2,1)} %all-gather.3.cloned.1.call-done, bf16[512,768]{1,0:T(8,128)(2,1)S(1)} %bitcast.156), kind=kOutput, calls=%fused_computation.11 | convolution fusion | flops 3731890176 | bytes 34507776 | tf_op jit(solution)/shard_map/dot_general | solution.py:83
  92.8 43.3 %all-gather.5.cloned.1.call-done = bf16[4704,512]{1,0:T(8,128)(2,1)} async-done(((bf16[1176,512]{1,0:T(8,128)(2,1)}), bf16[4704,512]{1,0:T(8,128)(2,1)}) %all-gather.5.cloned.1.call-update) | async-done | bytes 4816912 | tf_op jit(solution)/shard_map/all_gather | solution.py:112
  136.1 13.6 %convert_reduce_fusion.1 = (f32[4704]{0:T(1024)S(1)}, bf16[4704,384]{1,0:T(8,128)(2,1)}, f32[4704]{0:T(1024)S(1)}, f32[4704]{0:T(1024)S(1)}, f32[4704,384]{1,0:T(8,128)}) fusion(f32[4704,768]{1,0:T(8,128)} %get-tuple-element.80, bf16[4704,512]{1,0:T(8,128)(2,1)} %all-gather.5.cloned.1.call-done, f32[384,512]{1,0:T(8,128)S(1)} %copy-done.5), kind=kOutput, calls=%fused_computation.14 | convolution fusion | flops 1862514816 | bytes 30948480 | tf_op jit(solution)/shard_map/td,cd->tc/dot_general | solution.py:114
  169.4 16.2 %all-reduce.6 = (f32[4704]{0:T(1024)S(1)}, f32[4704]{0:T(1024)S(1)}) all-reduce(f32[4704]{0:T(1024)S(1)} %get-tuple-element.68, f32[4704]{0:T(1024)S(1)} %get-tuple-element.69), channel_id=1, replica_groups=mesh['dp'=8,'mp'=4] {'mp'}, use_global_device_ids=true, to_apply=%region_5.0 | all-reduce | flops 9408 | bytes 75264 | tf_op jit(solution)/shard_map/psum | solution.py:89
  185.6 8.6 multiply_reduce_fusion.1
  194.2 15.6 %all-reduce.5 = (f32[4704]{0:T(1024)S(1)}, f32[4704]{0:T(1024)S(1)}) all-reduce(f32[4704]{0:T(1024)S(1)} %get-tuple-element.21, f32[4704]{0:T(1024)S(1)} %reduce_sum.176), channel_id=1, replica_groups=mesh['dp'=8,'mp'=4] {'mp'}, use_global_device_ids=true, to_apply=%region_10.0 | all-reduce | flops 9408 | bytes 75264 | tf_op jit(solution)/shard_map/psum | solution.py:128
  209.9 12.3 %subtract_multiply_fusion = (f32[4704,384]{1,0:T(8,128)}, bf16[4704,384]{1,0:T(8,128)(2,1)}) fusion(f32[4704,384]{1,0:T(8,128)} %reshape.108, f32[4704]{0:T(1024)S(1)} %get-tuple-element.87, f32[4704]{0:T(1024)S(1)} %get-tuple-element.88, f32[384]{0:T(512)S(1)} %get-tuple-element.28, f32[4704]{0:T(1024)S(1)} %get-tuple-element.76, ...), kind=kLoop, calls=%fused_computation.16 | loop fusion | flops 18063360 | bytes 25367040 | tf_op jit(solution)/shard_map/mul | solution.py:129
  241.6 9.8 fusion.79
  252.3 13.4 %convert_reduce_fusion = (f32[768]{0:T(1024)}, bf16[4704,768]{1,0:T(8,128)(2,1)S(1)}) fusion(f32[4704,768]{1,0:T(8,128)} %get-tuple-element.81, f32[768]{0:T(1024)S(1)} %add.291, f32[4704,384]{1,0:T(8,128)S(1)} %bitcast.150, f32[4704,384]{1,0:T(8,128)S(1)} %get-tuple-element.70), kind=kLoop, calls=%fused_computation.10 | loop fusion | flops 86703360 | bytes 36132864 | tf_op jit(solution)/shard_map/reduce_sum | solution.py:136
  281.5 66.7 %all-reduce.22.cloned.1.call-done = (f32[512,2,384]{2,1,0:T(2,128)}, f32[384,512]{1,0:T(8,128)}) async-done(((f32[512,2,384]{2,1,0:T(2,128)}, f32[384,512]{1,0:T(8,128)}), (f32[512,2,384]{2,1,0:T(2,128)}, f32[384,512]{1,0:T(8,128)})) %all-reduce.22.cloned.1.call-update) | async-done | bytes 2359312 | tf_op jit(solution)/shard_map/psum | solution.py:163
  354.7 10.4 all-reduce.4
  374.9 66.9 %all-reduce.32.cloned.1.call-done = (f32[512,512]{1,0:T(8,128)}, f32[512,512]{1,0:T(8,128)}) async-done(((f32[512,512]{1,0:T(8,128)}, f32[512,512]{1,0:T(8,128)}), (f32[512,512]{1,0:T(8,128)}, f32[512,512]{1,0:T(8,128)})) %all-reduce.32.cloned.1.call-update) | async-done | bytes 2097168 | tf_op jit(solution)/shard_map/psum | solution.py:176
  460.2 69.9 %all-reduce.30.cloned.1.call-done = (f32[512,512]{1,0:T(8,128)}, f32[512,512]{1,0:T(8,128)}) async-done(((f32[512,512]{1,0:T(8,128)}, f32[512,512]{1,0:T(8,128)}), (f32[512,512]{1,0:T(8,128)}, f32[512,512]{1,0:T(8,128)})) %all-reduce.30.cloned.1.call-update) | async-done | bytes 2097168 | tf_op jit(solution)/shard_map/psum | solution.py:176
  548.0 70.0 %all-reduce.28.cloned.1.call-done = (f32[512,512]{1,0:T(8,128)}, f32[512,512]{1,0:T(8,128)}) async-done(((f32[512,512]{1,0:T(8,128)}, f32[512,512]{1,0:T(8,128)}), (f32[512,512]{1,0:T(8,128)}, f32[512,512]{1,0:T(8,128)})) %all-reduce.28.cloned.1.call-update) | async-done | bytes 2097168 | tf_op jit(solution)/shard_map/psum | solution.py:176
  640.0 64.9 %all-reduce.26.cloned.1.call-done = (f32[512,512]{1,0:T(8,128)}, f32[512,512]{1,0:T(8,128)}) async-done(((f32[512,512]{1,0:T(8,128)}, f32[512,512]{1,0:T(8,128)}), (f32[512,512]{1,0:T(8,128)}, f32[512,512]{1,0:T(8,128)})) %all-reduce.26.cloned.1.call-update) | async-done | bytes 2097168 | tf_op jit(solution)/shard_map/psum | solution.py:176
  724.9 10.9 fusion.81
  735.9 8.6 fusion.56
  756.1 17.4 %psum.162 = f32[4,384]{1,0:T(4,128)} all-reduce(f32[4,384]{1,0:T(4,128)} %pad_maximum_fusion.2), channel_id=1, replica_groups=mesh['dp'=8,'mp'=4] {'dp'}, use_global_device_ids=true, to_apply=%region_24.0 | all-reduce | flops 1536 | bytes 12288 | tf_op jit(solution)/shard_map/psum | solution.py:163
  774.9 59.1 %all-reduce.20.cloned.1.call-done = f32[196,196]{1,0:T(8,128)} async-done(((f32[196,196]{1,0:T(8,128)}), f32[196,196]{1,0:T(8,128)}) %all-reduce.20.cloned.1.call-update) | async-done | bytes 153680 | tf_op jit(solution)/shard_map/psum | solution.py:164
  844.8 63.6 %all-reduce.24.cloned.1.call-done = (f32[512,512]{1,0:T(8,128)}, f32[512,512]{1,0:T(8,128)}) async-done(((f32[512,512]{1,0:T(8,128)}, f32[512,512]{1,0:T(8,128)}), (f32[512,512]{1,0:T(8,128)}, f32[512,512]{1,0:T(8,128)})) %all-reduce.24.cloned.1.call-update) | async-done | bytes 2097168 | tf_op jit(solution)/shard_map/psum | solution.py:176
  928.6 79.8 %reduce-scatter.9.cloned.1.call-done = f32[1176,512]{1,0:T(8,128)} async-done(((f32[4704,512]{1,0:T(8,128)}), f32[1176,512]{1,0:T(8,128)}) %reduce-scatter.9.cloned.1.call-update) | async-done | bytes 2408464
  1011.4 97.1 %reduce-scatter.7.cloned.1.call-done = f32[1176,512]{1,0:T(8,128)} async-done(((f32[4704,512]{1,0:T(8,128)}), f32[1176,512]{1,0:T(8,128)}) %reduce-scatter.7.cloned.1.call-update) | async-done | bytes 2408464
  1112.8 39.5 %all-reduce.2 = (f32[3,512]{1,0:T(4,128)S(1)}, f32[196]{0:T(256)S(1)}) all-reduce(f32[3,512]{1,0:T(4,128)S(1)} %pad_maximum_fusion.1, f32[196]{0:T(256)S(1)} %copy-done.46), channel_id=1, replica_groups=mesh['dp'=8,'mp'=4] {'dp','mp'}, use_global_device_ids=true, to_apply=%region_20.0 | all-reduce | flops 1732 | bytes 13856 | tf_op jit(solution)/shard_map/psum | solution.py:164
  (227 shorter events, 214.4 us)
Async XLA Ops:
  7.2 69.1 %all-gather.3.cloned.1.call-start = ((), (), s32[]{:S(2)}) async-start(), calls=%async_computation.2 | async-start | bytes 6021120 | tf_op jit(solution)/shard_map/all_gather | solution.py:81
  15.6 120.5 %all-gather.5.cloned.1.call-start = ((), (), s32[]{:S(2)}) async-start(), calls=%async_computation.3 | async-start | bytes 6021120 | tf_op jit(solution)/shard_map/all_gather | solution.py:112
  16.3 332.0 %all-reduce.22.cloned.1.call-start = ((), (), s32[]{:S(2)}) async-start(), calls=%async_computation.7 | async-start | bytes 4718592 | tf_op jit(solution)/shard_map/psum | solution.py:163
  17.1 75.7 %copy-start.26 = (bf16[64,8,2,384]{3,1,2,0:T(8,128)(2,1)}, bf16[64,8,2,384]{3,1,2,0:T(8,128)(2,1)S(1)}, u32[]{:S(2)}) copy-start(bf16[64,8,2,384]{3,1,2,0:T(8,128)(2,1)S(1)} %copy.87) | copy-start | bytes 2359300
  76.3 59.8 %copy-start.5 = (f32[384,512]{1,0:T(8,128)S(1)}, f32[384,512]{1,0:T(8,128)}, u32[]{:S(2)}) copy-start(f32[384,512]{1,0:T(8,128)} %param.20) | copy-start | bytes 2359300
  274.8 73.5 %copy-start.25 = (f32[384,512]{1,0:T(8,128)S(1)}, f32[384,512]{1,0:T(8,128)}, u32[]{:S(2)}) copy-start(f32[384,512]{1,0:T(8,128)} %param.26) | copy-start | bytes 2359300
  281.3 69.7 %copy-start.23 = (f32[512,2,384]{2,1,0:T(2,128)S(1)}, f32[512,2,384]{2,1,0:T(2,128)}, u32[]{:S(2)}) copy-start(f32[512,2,384]{2,1,0:T(2,128)} %param.25) | copy-start | bytes 4718596
  281.3 160.5 %all-reduce.32.cloned.1.call-start = ((), (), s32[]{:S(2)}) async-start(), calls=%async_computation.12 | async-start | bytes 4194304 | tf_op jit(solution)/shard_map/psum | solution.py:176
  374.6 155.6 %all-reduce.30.cloned.1.call-start = ((), (), s32[]{:S(2)}) async-start(), calls=%async_computation.11 | async-start | bytes 4194304 | tf_op jit(solution)/shard_map/psum | solution.py:176
  374.9 72.7 %copy-start.19 = (f32[384,512]{1,0:T(8,128)S(1)}, f32[384,512]{1,0:T(8,128)}, u32[]{:S(2)}) copy-start(f32[384,512]{1,0:T(8,128)} %get-tuple-element.98) | copy-start | bytes 2359300
  460.2 157.8 %all-reduce.28.cloned.1.call-start = ((), (), s32[]{:S(2)}) async-start(), calls=%async_computation.10 | async-start | bytes 4194304 | tf_op jit(solution)/shard_map/psum | solution.py:176
  548.0 156.9 %all-reduce.26.cloned.1.call-start = ((), (), s32[]{:S(2)}) async-start(), calls=%async_computation.9 | async-start | bytes 4194304 | tf_op jit(solution)/shard_map/psum | solution.py:176
  634.9 199.1 %all-reduce.20.cloned.1.call-start = ((), (), s32[]{:S(2)}) async-start(), calls=%async_computation.4 | async-start | bytes 409600 | tf_op jit(solution)/shard_map/psum | solution.py:164
  639.9 268.5 %all-reduce.24.cloned.1.call-start = ((), (), s32[]{:S(2)}) async-start(), calls=%async_computation.8 | async-start | bytes 4194304 | tf_op jit(solution)/shard_map/psum | solution.py:176
  724.9 283.5 %reduce-scatter.9.cloned.1.call-start = ((), (), s32[]{:S(2)}) async-start(), calls=%async_computation.6 | async-start | bytes 12042240
  735.9 372.6 %reduce-scatter.7.cloned.1.call-start = ((), (), s32[]{:S(2)}) async-start(), calls=%async_computation.5 | async-start | bytes 12042240
  745.3 88.7 %copy-start.33 = (f32[196,196]{1,0:T(8,128)S(1)}, f32[196,196]{1,0:T(8,128)}, u32[]{:S(2)}) copy-start(f32[196,196]{1,0:T(8,128)} %param.27) | copy-start | bytes 460996
  925.8 82.6 %copy-start = (bf16[1176,512]{1,0:T(8,128)(2,1)S(1)}, bf16[1176,512]{1,0:T(8,128)(2,1)}, u32[]{:S(2)}) copy-start(bf16[1176,512]{1,0:T(8,128)(2,1)} %param.17) | copy-start | bytes 3612676
  925.8 82.6 %copy-start.32 = (f32[1176]{0:T(1024)S(1)}, f32[1176]{0:T(1024)}, u32[]{:S(2)}) copy-start(f32[1176]{0:T(1024)} %copy-done.31) | copy-start | bytes 14116
  925.8 82.6 %copy-start.35 = (f32[1176]{0:T(1024)S(1)}, f32[1176]{0:T(1024)}, u32[]{:S(2)}) copy-start(f32[1176]{0:T(1024)} %copy-done.34) | copy-start | bytes 14116
  925.8 82.6 %copy-start.37 = (f32[1,512]{1,0:T(1,128)S(1)}, f32[1,512]{1,0:T(1,128)}, u32[]{:S(2)}) copy-start(f32[1,512]{1,0:T(1,128)} %copy-done.36) | copy-start | bytes 6148
  928.6 179.9 %copy-start.13 = (bf16[1176,512]{1,0:T(8,128)(2,1)S(1)}, bf16[1176,512]{1,0:T(8,128)(2,1)}, u32[]{:S(2)}) copy-start(bf16[1176,512]{1,0:T(8,128)(2,1)} %param.18) | copy-start | bytes 3612676
  928.6 179.9 %copy-start.40 = (f32[1,512]{1,0:T(1,128)S(1)}, f32[1,512]{1,0:T(1,128)}, u32[]{:S(2)}) copy-start(f32[1,512]{1,0:T(1,128)} %get-tuple-element.77) | copy-start | bytes 6148
  1112.7 44.8 %copy-start.24 = (f32[196,196]{1,0:T(8,128)S(1)}, f32[196,196]{1,0:T(8,128)}, u32[]{:S(2)}) copy-start(f32[196,196]{1,0:T(8,128)} %all-reduce.20.cloned.1.call-done) | copy-start | bytes 460996
  (42 other events, 541.4 us)
Sparse Core Ops, SparseCore 0:
  15.7 60.5 all-gather.2
  78.1 57.8 all-gather.4
  281.4 66.7 all-reduce.21
  374.7 67.1 all-reduce.31
  460.3 69.8 all-reduce.29
  548.1 69.8 all-reduce.27
  635.0 69.8 all-reduce.25
  711.0 122.9 all-reduce.19
  837.6 70.7 all-reduce.23
  911.7 96.6 reduce-scatter.8
  1011.8 96.6 reduce-scatter.6
where the time goes:
time: 1170 us; the launch traced here: 1160 us
  waiting for transfers between devices  741 us (63%)
  matrix products  179 us (15%)
  blocking collectives  99.3 us (8%)
  other arithmetic  78.7 us (7%)
  local copies, waits for them, and re-layouts  49.1 us (4%)
  between operations  17 us (1%)
    psum x5, waiting for transfers between devices, per_device(): lax.psum((jnp.dot(ortho_in, ortho_in.T, precision=HIGHEST), jnp.dot(ortho...  335 us
    unnamed x13, waiting for transfers between devices  178 us
    psum x1, waiting for transfers between devices, per_device(): lax.psum((grad_w_in, grad_w_out, gate_part), 'dp')  66.7 us
    all_gather x1, waiting for transfers between devices, per_device(): gathered = lax.all_gather(normed, 'mp', axis=0, tiled=True)  59.2 us
    psum x1, waiting for transfers between devices, per_device(): lax.psum((grad_spatial, grad_patch, model_part), ('dp', 'mp'))  59.1 us
    all_gather x1, waiting for transfers between devices, per_device(): cot_all = lax.all_gather(cotangent, 'mp', axis=0, tiled=True)  43.3 us
    psum x1, blocking collectives, per_device(): lax.psum((grad_spatial, grad_patch, model_part), ('dp', 'mp'))  39.5 us
    dot_general x15, matrix products, newton_step(): jnp.dot(gram, gram, precision=HIGHEST)  32.5 us
  transfers between devices with their start and end apart: 11, of which 11 were waited for; matrix products, arithmetic and copies ran while one was open for 9% of the time, Pallas kernels for 0%

commit v1 on v0

v1 whole, which is shorter than its diff:
```python
import functools
import math

import jax
import jax.numpy as jnp
from jax import lax
from jax.experimental import pallas as pl
from jax.experimental.pallas import tpu as pltpu
from jax.sharding import PartitionSpec as P

STEP = 10
EPSILON = 1e-05
HIGHEST = lax.Precision.HIGHEST
COEF_FIRST = 3.4445
COEF_SECOND = -4.775
COEF_THIRD = 2.0315
MOMENTUM = 0.95
MUON_RATE = 0.2
ADAM_RATE = 0.3
DECAY_RATE = 0.01
BETA_FIRST = 0.9
BETA_SECOND = 0.95
LOW = jnp.bfloat16
F32 = jnp.float32


ROW_TILE = 16
CUBIC = 0.044715
SLOPE = math.sqrt(2.0 / math.pi)


def compiler(megabytes):
    return pltpu.CompilerParams(vmem_limit_bytes=megabytes << 20)


def dot_nn(a, b):
    return jnp.dot(a, b, preferred_element_type=F32)


def dot_nt(a, b):
    return lax.dot_general(a, b, (((1,), (1,)), ((), ())), preferred_element_type=F32)


def gelu_pair(hidden):
    square = hidden * hidden
    half = 0.5 + 0.5 * jnp.tanh(hidden * (SLOPE + (SLOPE * CUBIC) * square))
    active = hidden * half
    slope = half + (active - active * half) * (2.0 * SLOPE + (6.0 * SLOPE * CUBIC) * square)
    return active, slope


def lanes(v):
    total = v[:, :128]
    for at in range(128, v.shape[1], 128):
        total = total + v[:, at : at + 128]
    return total


def eights(v):
    total = v[:8]
    for at in range(8, v.shape[0], 8):
        total = total + v[at : at + 8]
    return total


def tiles(count, body, carry=None):
    def step(i, kept):
        return body(pl.ds(pl.multiple_of(i * ROW_TILE, ROW_TILE), ROW_TILE), kept)

    return lax.fori_loop(0, count // ROW_TILE, step, carry, unroll=False)


def gate_kernel(chunk, normed, weight, vec, normal, unit, slope, scale, active):
    rows, full = active.shape
    starts = range(0, full, chunk)
    for at in starts:
        active[:, at : at + chunk] = dot_nn(normed[...], weight[:, at : at + chunk])

    def act(here, _):
        total = jnp.zeros((ROW_TILE, 128), F32)
        for at in starts:
            cols = slice(at, at + chunk)
            value, grad = gelu_pair(active[here, cols] + vec[1:2, cols])
            active[here, cols] = value
            slope[here, cols] = grad.astype(LOW)
            total = total + lanes(value)
        scale[here, :] = total

    tiles(rows, act)
    mean = jnp.sum(scale[...], axis=1, keepdims=True) * (1.0 / full)
    scale[...] = jnp.broadcast_to(mean, scale.shape)

    def spread(here, _):
        total = jnp.zeros((ROW_TILE, 128), F32)
        mean_here = scale[here, :][:, :1]
        for at in starts:
            cols = slice(at, at + chunk)
            centred = active[here, cols] - mean_here
            active[here, cols] = centred
            total = total + lanes(centred * centred)
        scale[here, :] = total

    tiles(rows, spread)
    var = jnp.sum(scale[...], axis=1, keepdims=True) * (1.0 / full)
    scale[...] = jnp.broadcast_to(lax.rsqrt(var + EPSILON), scale.shape)

    def finish(here, _):
        inv = scale[here, :][:, :1]
        for at in starts:
            cols = slice(at, at + chunk)
            unit_here = active[here, cols] * inv
            unit[here, cols] = unit_here.astype(LOW)
            normal[here, cols] = (unit_here * vec[2:3, cols] + vec[3:4, cols]).astype(LOW)

    tiles(rows, finish)


def gate_forward(normed, weight, vec, images, pad):
    width, full = weight.shape
    chunk = 512 if full % 512 == 0 else full
    total = images * pad
    whole = lambda shape: pl.BlockSpec(shape, lambda i: (0, 0))
    rows = lambda n: pl.BlockSpec((pad, n), lambda i: (i, 0))
    return pl.pallas_call(
        functools.partial(gate_kernel, chunk),
        grid=(images,),
        in_specs=[rows(width), whole((width, full)), whole(vec.shape)],
        out_specs=[rows(full), rows(full), rows(full), rows(128)],
        out_shape=[jax.ShapeDtypeStruct((total, full), LOW)] * 3
        + [jax.ShapeDtypeStruct((total, 128), F32)],
        scratch_shapes=[pltpu.VMEM((pad, full), F32)],
        compiler_params=compiler(48),
        cost_estimate=pl.CostEstimate(
            flops=2 * total * width * full, bytes_accessed=8 * total * full, transcendentals=total * full
        ),
        name="gate_forward",
    )(normed, weight, vec)


def value_kernel(
    pad,
    images,
    core,
    normed,
    cot,
    normed_t,
    cot_t,
    normal,
    unit,
    w_value,
    w_back,
    mix,
    mix_t,
    bias,
    vec,
    gated,
    low_value,
    grad_unit,
    mine_value,
    theirs_value,
    mine_out,
    theirs_out,
    sum_one,
    sum_two,
    grad_mix,
    grad_bias,
    columns,
    hidden,
    back,
    mixed,
    low_mixed,
    low_pad,
    gated_pad,
):
    total, chunk = hidden.shape
    half = mine_value.shape[0]
    step = pl.program_id(0)

    @pl.when(step == 0)
    def _():
        sum_one[...] = jnp.zeros_like(sum_one)
        sum_two[...] = jnp.zeros_like(sum_two)
        grad_mix[...] = jnp.zeros_like(grad_mix)
        grad_bias[...] = jnp.zeros_like(grad_bias)
        low_pad[total:, :] = jnp.zeros_like(low_pad[total:, :])
        gated_pad[total:, :] = jnp.zeros_like(gated_pad[total:, :])

    hidden[...] = dot_nn(normed[...], w_value[...])
    back[...] = dot_nn(cot[...], w_back[...])
    for image in range(images):
        here = slice(image * pad, (image + 1) * pad)
        mixed[here, :] = dot_nn(mix[...], normal[here, :])

    def forward(i, sums):
        here = pl.ds(pl.multiple_of(i * ROW_TILE, ROW_TILE), ROW_TILE)
        row = pl.ds(pl.multiple_of(lax.rem(i, pad // ROW_TILE) * ROW_TILE, ROW_TILE), ROW_TILE)
        value, slope = gelu_pair(hidden[here, :] + vec[0:1, :])
        mixed_here = mixed[here, :] + bias[row, :][:, :1]
        back_here = back[here, :]
        gated_here = (value * mixed_here).astype(LOW)
        gated[here, :] = gated_here
        gated_pad[here, :] = gated_here
        grad_here = (back_here * value).astype(LOW)
        low_mixed[here, :] = grad_here
        grad_bias[row, :] += lanes(grad_here.astype(F32))
        low_here = (back_here * mixed_here * slope).astype(LOW)
        low_value[here, :] = low_here
        low_pad[here, :] = low_here
        return sums + eights(low_here.astype(F32))

    bias_sum = lax.fori_loop(0, total // ROW_TILE, forward, jnp.zeros((8, chunk), F32))

    for image in range(images):
        here = slice(image * pad, (image + 1) * pad)
        mixed[here, :] = dot_nn(mix_t[...], low_mixed[here, :])
        grad_mix[...] += dot_nt(low_mixed[here, :], normal[here, :])

    first = pl.multiple_of(core[0] * half, half)
    other = pl.multiple_of((1 - core[0]) * half, half)
    mine_value[...] = dot_nn(normed_t[pl.ds(first, half), :], low_pad[...])
    theirs_value[...] = dot_nn(normed_t[pl.ds(other, half), :], low_pad[...]).astype(LOW)
    mine_out[...] = dot_nn(cot_t[pl.ds(first, half), :], gated_pad[...])
    theirs_out[...] = dot_nn(cot_t[pl.ds(other, half), :], gated_pad[...]).astype(LOW)

    def backward(i, sums):
        here = pl.ds(pl.multiple_of(i * ROW_TILE, ROW_TILE), ROW_TILE)
        grad = mixed[here, :]
        unit_here = unit[here, :].astype(F32)
        gain = vec[2:3, :]
        both = grad * unit_here
        du = grad * gain
        grad_unit[here, :] = du.astype(LOW)
        sum_one[here, :] += lanes(du)
        sum_two[here, :] += lanes(both * gain)
        return sums[0] + eights(both), sums[1] + eights(grad)

    zero = jnp.zeros((8, chunk), F32)
    gain_sum, shift_sum = lax.fori_loop(0, total // ROW_TILE, backward, (zero, zero))
    columns[0:8, :] = bias_sum
    columns[8:16, :] = gain_sum
    columns[16:24, :] = shift_sum


def value_both(core, normed, cot, normed_t, cot_t, normal, unit, w_value, w_back, mix, mix_t, bias, vec, images, pad):
    width, full = w_value.shape
    total = images * pad
    deep = normed_t.shape[1]
    chunk = 512 if full % 512 == 0 else full
    half = width // 2
    once = pl.Buffered(1)
    whole = lambda a: pl.BlockSpec(a.shape, lambda i, c: (0, 0), pipeline_mode=once)
    cols = lambda n: pl.BlockSpec((n, chunk), lambda i, c: (0, i))
    fixed = lambda *s: pl.BlockSpec(s, lambda i, c: (0, 0))
    shape = jax.ShapeDtypeStruct
    return pl.pallas_call(
        functools.partial(value_kernel, pad, images),
        grid_spec=pltpu.PrefetchScalarGridSpec(
            num_scalar_prefetch=1,
            grid=(full // chunk,),
            in_specs=[whole(normed), whole(cot), whole(normed_t), whole(cot_t)]
            + [cols(total), cols(total), cols(width), cols(width)]
            + [whole(mix), whole(mix_t), whole(bias), cols(4)],
            out_specs=[cols(total), cols(total), cols(total)]
            + [cols(half)] * 4
            + [fixed(total, 128), fixed(total, 128), fixed(pad, pad), fixed(pad, 128), cols(24)],
            scratch_shapes=[pltpu.VMEM((total, chunk), F32)] * 3
            + [pltpu.VMEM((total, chunk), LOW)]
            + [pltpu.VMEM((deep, chunk), LOW)] * 2,
        ),
        out_shape=[shape((total, full), LOW)] * 3
        + [shape((half, full), F32), shape((half, full), LOW)] * 2
        + [shape((total, 128), F32)] * 2
        + [shape((pad, pad), F32), shape((pad, 128), F32), shape((24, full), F32)],
        compiler_params=compiler(60),
        cost_estimate=pl.CostEstimate(
            flops=12 * total * width * full, bytes_accessed=20 * total * full, transcendentals=total * full
        ),
        name="value_both",
    )(core, normed, cot, normed_t, cot_t, normal, unit, w_value, w_back, mix, mix_t, bias, vec)


def gate_back_kernel(
    full, core, normed_t, grad_unit, unit, slope, scale, sum_one, sum_two, low_gate, mine, theirs, columns, means, low_pad
):
    total, chunk = low_gate.shape
    half = mine.shape[0]

    @pl.when(pl.program_id(0) == 0)
    def _():
        first = jnp.sum(sum_one[...], axis=1, keepdims=True) * (1.0 / full)
        means[0] = jnp.broadcast_to(first, (total, 128))
        second = jnp.sum(sum_two[...], axis=1, keepdims=True) * (1.0 / full)
        means[1] = jnp.broadcast_to(second, (total, 128))
        low_pad[total:, :] = jnp.zeros_like(low_pad[total:, :])

    def back(i, sums):
        here = pl.ds(pl.multiple_of(i * ROW_TILE, ROW_TILE), ROW_TILE)
        one = means[0, here, :][:, :1]
        two = means[1, here, :][:, :1]
        inv = scale[here, :][:, :1]
        grad = inv * (grad_unit[here, :].astype(F32) - one - unit[here, :].astype(F32) * two)
        low = (grad * slope[here, :].astype(F32)).astype(LOW)
        low_gate[here, :] = low
        low_pad[here, :] = low
        return sums + eights(low.astype(F32))

    columns[...] = lax.fori_loop(0, total // ROW_TILE, back, jnp.zeros((8, chunk), F32))
    first = pl.multiple_of(core[0] * half, half)
    other = pl.multiple_of((1 - core[0]) * half, half)
    mine[...] = dot_nn(normed_t[pl.ds(first, half), :], low_pad[...])
    theirs[...] = dot_nn(normed_t[pl.ds(other, half), :], low_pad[...]).astype(LOW)


def gate_back(core, normed_t, grad_unit, unit, slope, scale, sum_one, sum_two):
    total, full = unit.shape
    width, deep = normed_t.shape
    chunk = 512 if full % 512 == 0 else full
    half = width // 2
    whole = lambda a: pl.BlockSpec(a.shape, lambda i, c: (0, 0), pipeline_mode=pl.Buffered(1))
    cols = lambda n: pl.BlockSpec((n, chunk), lambda i, c: (0, i))
    shape = jax.ShapeDtypeStruct
    return pl.pallas_call(
        functools.partial(gate_back_kernel, full),
        grid_spec=pltpu.PrefetchScalarGridSpec(
            num_scalar_prefetch=1,
            grid=(full // chunk,),
            in_specs=[whole(normed_t), cols(total), cols(total), cols(total)]
            + [whole(scale), whole(sum_one), whole(sum_two)],
            out_specs=[cols(total), cols(half), cols(half), cols(8)],
            scratch_shapes=[pltpu.VMEM((2, total, 128), F32), pltpu.VMEM((deep, chunk), LOW)],
        ),
        out_shape=[
            shape((total, full), LOW),
            shape((half, full), F32),
            shape((half, full), LOW),
            shape((8, full), F32),
        ],
        compiler_params=compiler(48),
        cost_estimate=pl.CostEstimate(
            flops=2 * total * width * full, bytes_accessed=10 * total * full, transcendentals=0
        ),
        name="gate_back",
    )(core, normed_t, grad_unit, unit, slope, scale, sum_one, sum_two)


def token_kernel(tokens, cot, gated, low_value, low_gate, w_value, w_gate, w_back, model, output, grad_tokens, sums):
    @pl.when(pl.program_id(0) == 0)
    def _():
        sums[...] = jnp.zeros_like(sums)

    rows = tokens[...].astype(F32)
    width = rows.shape[1]
    branch = dot_nt(gated[...], w_back[...])
    output[...] = (rows + branch + model[2:3, :]).astype(LOW)
    grad = dot_nt(low_value[...], w_value[...]) + dot_nt(low_gate[...], w_gate[...])
    mean = jnp.sum(rows, axis=1, keepdims=True) * (1.0 / width)
    centred = rows - mean
    var = jnp.sum(centred * centred, axis=1, keepdims=True) * (1.0 / width)
    inv = lax.rsqrt(var + EPSILON)
    unit = centred * inv
    both = grad * unit
    du = grad * model[0:1, :]
    first = jnp.sum(du, axis=1, keepdims=True) * (1.0 / width)
    second = jnp.sum(both * model[0:1, :], axis=1, keepdims=True) * (1.0 / width)
    cot_here = cot[...].astype(F32)
    grad_tokens[...] = (cot_here + inv * (du - first - unit * second)).astype(LOW)
    sums[0:8, :] += eights(both)
    sums[8:16, :] += eights(grad)
    sums[16:24, :] += eights(cot_here)


def token_back(tokens, cot, gated, low_value, low_gate, w_value, w_gate, w_back, model, images, pad):
    width, full = w_value.shape
    total = images * pad
    rows = lambda n: pl.BlockSpec((pad, n), lambda i: (i, 0))
    whole = lambda a: pl.BlockSpec(a.shape, lambda i: (0, 0), pipeline_mode=pl.Buffered(1))
    shape = jax.ShapeDtypeStruct
    return pl.pallas_call(
        token_kernel,
        grid=(images,),
        in_specs=[rows(width), rows(width), rows(full), rows(full), rows(full)]
        + [whole(w_value), whole(w_gate), whole(w_back), whole(model)],
        out_specs=[rows(width), rows(width), pl.BlockSpec((24, width), lambda i: (0, 0))],
        out_shape=[shape((total, width), LOW), shape((total, width), LOW), shape((24, width), F32)],
        compiler_params=compiler(48),
        cost_estimate=pl.CostEstimate(
            flops=6 * total * width * full, bytes_accessed=8 * total * full, transcendentals=0
        ),
        name="token_back",
    )(tokens, cot, gated, low_value, low_gate, w_value, w_gate, w_back, model)


def split_two(v):
    high = v.astype(LOW)
    return high, (v - high.astype(F32)).astype(LOW)


def dot3(a, b):
    return dot_nn(a[0], b[0]) + (dot_nn(a[0], b[1]) + dot_nn(a[1], b[0]))


def muon_kernel(moments, mine, ortho, gram_now, total):
    size = gram_now.shape[0]
    gram = dot_nt(moments[...], moments[...])
    row = lax.broadcasted_iota(jnp.int32, (size, size), 0)
    col = lax.broadcasted_iota(jnp.int32, (size, size), 1)
    same = row == col
    norm = jnp.sqrt(jnp.sum(jnp.where(same, gram, 0.0), keepdims=True)) + 1e-07
    inv = 1.0 / norm
    gram_now[...] = gram * (inv * inv)
    for sweep in range(5):
        now = gram_now[...]
        now_two = split_two(now)
        extra = COEF_SECOND * now + COEF_THIRD * dot3(now_two, now_two)
        extra_two = split_two(extra)
        if sweep == 0:
            total[...] = jnp.where(same, COEF_FIRST + extra, extra)
        else:
            total[...] = COEF_FIRST * total[...] + dot3(extra_two, split_two(total[...]))
        if sweep < 4:
            half = COEF_FIRST * now + dot3(extra_two, now_two)
            gram_now[...] = COEF_FIRST * half + dot3(extra_two, split_two(half))
    ortho[...] = dot3(split_two(total[...]), split_two(mine[...])) * inv


def muon(moments, mine):
    size, full = moments.shape
    return pl.pallas_call(
        muon_kernel,
        out_shape=jax.ShapeDtypeStruct(mine.shape, F32),
        scratch_shapes=[pltpu.VMEM((size, size), F32)] * 2,
        compiler_params=compiler(48),
        cost_estimate=pl.CostEstimate(
            flops=2 * size * size * (51 * size + full), bytes_accessed=8 * size * full, transcendentals=0
        ),
        name="muon",
    )(moments, mine)
def newton_step(ortho, gram):
    polynomial = COEF_SECOND * gram + COEF_THIRD * jnp.dot(gram, gram, precision=HIGHEST)
    return COEF_FIRST * ortho + jnp.dot(polynomial, ortho, precision=HIGHEST)


def orthogonal(moment):
    ortho = moment / (jnp.sqrt(jnp.sum(moment * moment)) + 1e-07)
    for sweep in range(5):
        ortho = newton_step(ortho, jnp.dot(ortho, ortho.T, precision=HIGHEST))
    return ortho


def adam_update(param_now, grad_now, first_old, second_old):
    first_new = BETA_FIRST * first_old + (1.0 - BETA_FIRST) * grad_now
    second_new = BETA_SECOND * second_old + (1.0 - BETA_SECOND) * grad_now * grad_now
    first_hat = first_new / (1.0 - BETA_FIRST**STEP)
    second_hat = second_new / (1.0 - BETA_SECOND**STEP)
    updated = param_now * (1.0 - ADAM_RATE * DECAY_RATE) - ADAM_RATE * first_hat / (
        jnp.sqrt(second_hat) + 1e-08
    )
    return (second_new, updated)


def core_index():
    return lax.axis_index("dp") % 2


def swap_core(part):
    return lax.ppermute(part, "dp", [(i, i ^ 1) for i in range(lax.axis_size("dp"))])


def both_cores(mine):
    theirs = swap_core(mine)
    first = core_index() == 0
    return jnp.concatenate([jnp.where(first, mine, theirs), jnp.where(first, theirs, mine)], axis=0)


def exchange_mp(parts):
    return lax.all_to_all(parts, "mp", 0, 0)


def exchange_z(parts):
    size = lax.axis_size("dp")
    groups = [list(range(c, size, 2)) for c in range(2)]
    return lax.all_to_all(parts, "dp", 0, 0, axis_index_groups=groups)


def copies(part, count):
    return jnp.broadcast_to(part[None], (count,) + part.shape)


def gather_mp(part):
    return exchange_mp(copies(part, lax.axis_size("mp")))


def core_rows(rows, core):
    half = rows.shape[0] // 2
    return lax.dynamic_slice_in_dim(rows, core * half, half, 0)


def high_low(v):
    high = lax.reduce_precision(v, 8, 7)
    return high.astype(LOW), (v - high).astype(LOW)


def to_wire(main, small):
    return jnp.concatenate([main.astype(LOW), *high_low(small)], axis=-1)


def from_wire(wire, extra):
    cut = wire.shape[-1] - 2 * extra
    main, high, low = jnp.split(wire, [cut, cut + extra], axis=-1)
    return main.astype(F32), high.astype(F32) + low.astype(F32)


def plane_sum(mine, theirs, small):
    ways = lax.axis_size("mp")
    rows = mine[0].shape[0]
    mains = []
    for own, other in zip(mine, theirs):
        both = own + swap_core(other).astype(F32)
        mains.append(both.reshape(rows, ways, -1).transpose(1, 0, 2))
    main = jnp.concatenate(mains, axis=2)
    if small is None:
        return jnp.sum(exchange_mp(main.astype(LOW)).astype(F32), axis=0), None
    core = core_index()
    other = core_rows(small, 1 - core)
    got = swap_core(jnp.stack(high_low(other))).astype(F32)
    both = core_rows(small, core) + (got[0] + got[1])
    both = both.reshape(rows, ways, -1).transpose(1, 0, 2)
    parts, smalls = from_wire(exchange_mp(to_wire(main, both)), both.shape[2])
    return jnp.sum(parts, axis=0), jnp.sum(smalls, axis=0)


def depth_sum(main, small):
    depth = lax.axis_size("dp") // 2
    rows = main.shape[0]
    extra = small.shape[1]
    wire = to_wire(main, small).reshape(depth, rows // depth, -1)
    parts, smalls = from_wire(exchange_z(wire), extra)
    wire = to_wire(jnp.sum(parts, axis=0), jnp.sum(smalls, axis=0))
    wire = exchange_z(copies(wire, depth)).reshape(rows, -1)
    return from_wire(wire, extra)


def depth_exchange(main):
    depth = lax.axis_size("dp") // 2
    return jnp.sum(exchange_z(copies(main.astype(LOW), depth)).astype(F32), axis=0)


def to_images(rows, patches, count, pad):
    here, width = rows.shape
    spare = count * patches - here
    if spare:
        odd = lax.axis_index("mp") % 2 == 1
        size = lax.axis_size("mp")
        got = lax.ppermute(rows[:spare], "mp", [(i, i - 1) for i in range(1, size, 2)])
        kept = jnp.concatenate([rows[spare:], jnp.zeros((2 * spare, width), rows.dtype)], axis=0)
        rows = jnp.where(odd, kept, jnp.concatenate([rows, got], axis=0))
    images = rows.reshape(count, patches, width)
    return jnp.pad(images, ((0, 0), (0, pad - patches), (0, 0))).reshape(count * pad, width)


def from_images(rows, patches, count, pad, here):
    width = rows.shape[1]
    rows = rows.reshape(count, pad, width)[:, :patches].reshape(count * patches, width)
    spare = count * patches - here
    if spare:
        odd = lax.axis_index("mp") % 2 == 1
        size = lax.axis_size("mp")
        got = lax.ppermute(rows[here:], "mp", [(i, i + 1) for i in range(0, size, 2)])
        kept = jnp.concatenate([got, rows[: here - spare]], axis=0)
        rows = jnp.where(odd, kept, rows[:here])
    return rows


def per_device(
    tokens,
    cotangent,
    w_in,
    w_out,
    spatial,
    model_vectors,
    gate_vectors,
    patch_bias,
    moment_in,
    moment_out,
    moment_mix,
    first_model,
    second_model,
    first_gate,
    second_gate,
    first_patch,
    second_patch,
):
    here, width = tokens.shape
    shard = w_in.shape[2]
    ways = lax.axis_size("mp")
    full = shard * ways
    patches = spatial.shape[0]
    images = -(-here // patches)
    pad = -(-patches // 16) * 16
    total = images * pad
    deep = -(-total // 128) * 128
    core = core_index()
    core_arg = core.astype(jnp.int32).reshape(1)

    vec_all = gather_mp(gate_vectors).transpose(1, 0, 2).reshape(4, full)
    gate_part = gather_mp(core_rows(w_in[:, 1], core).astype(LOW))
    w_gate = both_cores(gate_part.transpose(1, 0, 2).reshape(width // 2, full))
    rest = jnp.concatenate([core_rows(w_in[:, 0], core), core_rows(w_out.T, core)], axis=1)
    rest = gather_mp(rest.astype(LOW))
    rest = jnp.stack([rest[:, :, :shard], rest[:, :, shard:]]).transpose(2, 0, 1, 3)
    rest = both_cores(rest.reshape(width // 2, 2 * full))
    w_value, w_back = rest[:, :full], rest[:, full:]

    tokens_pad = to_images(tokens, patches, images, pad)
    cot_pad = to_images(cotangent, patches, images, pad)
    rows_in = tokens_pad.astype(F32)
    centred = rows_in - jnp.mean(rows_in, axis=1, keepdims=True)
    inv_in = lax.rsqrt(jnp.mean(centred * centred, axis=1, keepdims=True) + EPSILON)
    normed = (centred * inv_in * model_vectors[0] + model_vectors[1]).astype(LOW)
    normed_t = jnp.pad(normed.T, ((0, 0), (0, deep - total)))
    cot_t = jnp.pad(cot_pad.T, ((0, 0), (0, deep - total)))
    mix = jnp.pad(spatial.astype(LOW), ((0, pad - patches), (0, pad - patches)))
    bias = jnp.broadcast_to(jnp.pad(patch_bias, (0, pad - patches))[:, None], (pad, 128))

    normal, unit, slope, scale = gate_forward(normed, w_gate, vec_all, images, pad)
    (
        gated,
        low_value,
        grad_unit,
        mine_value,
        theirs_value,
        mine_out,
        theirs_out,
        sum_one,
        sum_two,
        grad_mix,
        grad_bias,
        columns,
    ) = value_both(
        core_arg, normed, cot_pad, normed_t, cot_t, normal, unit, w_value, w_back, mix, mix.T, bias, vec_all, images, pad
    )
    low_gate, mine_gate, theirs_gate, gate_columns = gate_back(
        core_arg, normed_t, grad_unit, unit, slope, scale, sum_one, sum_two
    )
    output, grad_tokens, model_sums = token_back(
        tokens_pad, cot_pad, gated, low_value, low_gate, w_value, w_gate, w_back, model_vectors, images, pad
    )

    grad_vec = jnp.stack(
        [
            jnp.sum(columns[0:8], axis=0),
            jnp.sum(gate_columns, axis=0),
            jnp.sum(columns[8:16], axis=0),
            jnp.sum(columns[16:24], axis=0),
        ]
    )
    grad_model = jnp.sum(model_sums.reshape(3, 8, width), axis=1)
    grad_patch = jnp.sum(grad_bias[:patches], axis=1)
    flat = [grad_mix[:patches, :patches], grad_patch, grad_model, grad_vec]
    sizes = [math.prod(f.shape) for f in flat]
    unit_size = width * ways
    padded = -(-sum(sizes) // unit_size) * unit_size
    small = jnp.concatenate([f.reshape(-1) for f in flat] + [jnp.zeros(padded - sum(sizes), F32)])
    small = small.reshape(width, padded // width)
    extra = padded // unit_size

    main_one, small_one = plane_sum((mine_value, mine_out), (theirs_value, theirs_out), small)
    main_one, small_one = depth_sum(main_one, small_one)
    main_two, _ = plane_sum((mine_gate,), (theirs_gate,), None)
    main_two = depth_exchange(main_two)

    old_one = jnp.concatenate([moment_in[:, 0], moment_out.T], axis=1)
    half_one = MOMENTUM * core_rows(old_one, core) + main_one
    wire_one = gather_mp(to_wire(half_one, small_one))
    wire_one = both_cores(wire_one.transpose(1, 0, 2))
    grads_one = both_cores(main_one)
    half_two = MOMENTUM * core_rows(moment_in[:, 1], core) + main_two
    wire_two = gather_mp(half_two.astype(LOW))
    wire_two = both_cores(wire_two.transpose(1, 0, 2).reshape(width // 2, full))
    grads_two = both_cores(main_two)

    _, small = from_wire(wire_one, extra)
    small = small.reshape(-1)
    ends = [sum(sizes[: i + 1]) for i in range(4)]
    grad_spatial = small[: ends[0]].reshape(patches, patches)
    grad_patch = small[ends[0] : ends[1]]
    grad_model = small[ends[1] : ends[2]].reshape(3, width)
    grad_vec = small[ends[2] : ends[3]].reshape(4, full)
    grad_vec = lax.dynamic_slice_in_dim(grad_vec, lax.axis_index("mp") * shard, shard, 1)

    all_value = wire_one[:, :, :shard].reshape(width, full)
    all_out = wire_one[:, :, shard : 2 * shard].reshape(width, full)
    moment_out_t = MOMENTUM * moment_out.T + grads_one[:, shard:]
    ortho_out = muon(all_out, moment_out_t).T
    grad_in = jnp.concatenate([grads_one[:, :shard], grads_two], axis=1)
    moment_in_flat = MOMENTUM * moment_in.reshape(width, 2 * shard) + grad_in
    ortho_in = muon(jnp.concatenate([all_value, wire_two], axis=1), moment_in_flat)
    ortho_in = ortho_in.reshape(width, 2, shard)
    new_moment_in = moment_in_flat.reshape(width, 2, shard)
    new_moment_out = moment_out_t.T
    grad_w_in = grad_in.reshape(width, 2, shard)
    grad_w_out = grads_one[:, shard:].T
    new_moment_mix = MOMENTUM * moment_mix + grad_spatial

    shrink_by = 1.0 - MUON_RATE * DECAY_RATE
    new_w_in = w_in * shrink_by - MUON_RATE * 0.2 * math.sqrt(max(width, 2 * full)) * ortho_in
    new_w_out = w_out * shrink_by - MUON_RATE * 0.2 * math.sqrt(max(width, full)) * ortho_out
    new_spatial = spatial * shrink_by - MUON_RATE * 0.2 * math.sqrt(patches) * orthogonal(
        new_moment_mix
    )
    new_second_model, new_model = adam_update(model_vectors, grad_model, first_model, second_model)
    new_second_gate, new_gate = adam_update(gate_vectors, grad_vec, first_gate, second_gate)
    new_second_patch, new_patch = adam_update(patch_bias, grad_patch, first_patch, second_patch)
    return (
        from_images(output, patches, images, pad, here),
        from_images(grad_tokens, patches, images, pad, here),
        grad_w_in,
        grad_w_out,
        grad_spatial,
        grad_model,
        grad_vec,
        grad_patch,
        new_moment_in,
        new_moment_out,
        new_moment_mix,
        new_second_model,
        new_second_gate,
        new_second_patch,
        new_w_in,
        new_w_out,
        new_spatial,
        new_model,
        new_gate,
        new_patch,
    )


def solution(mesh):
    rows = P(("dp", "mp"), None)
    wide = P(None, None, "mp")
    tall = P("mp", None)
    columns = P(None, "mp")
    return jax.shard_map(
        per_device,
        mesh=mesh,
        in_specs=(
            (rows, rows, wide, tall, P(), P(), columns, P())
            + (wide, tall, P(), P(), P(), columns, columns, P(), P())
        ),
        out_specs=(
            (rows, rows, wide, tall, P(), P(), columns, P())
            + (wide, tall, P(), P(), columns, P())
            + (wide, tall, P(), P(), columns, P())
        ),
        check_vma=False,
    )
```

time: 1170 us -> 465 us (0.40)
  waiting for transfers between devices: 741 us -> 119 us
  matrix products: 179 us -> 5.77 us
  Pallas kernels: 0 us -> 145 us
  blocking collectives: 99.3 us -> 0 us
  local copies, waits for them, and re-layouts: 49.1 us -> 92 us
  starting transfers between devices: 0.84 us -> 42.2 us
  other arithmetic: 78.7 us -> 51.4 us
  between operations: 17 us -> 2.59 us
    psum x7 -> x0, waiting for transfers between devices: 461 us -> none  [the longest x5 335 us: per_device(): lax.psum((jnp.dot(ortho_in, ortho_in.T, precision=HIGHEST), jnp.dot(ortho...]
    unnamed x13 -> x0, waiting for transfers between devices: 178 us -> none
    pallas_call x0 -> x6, Pallas kernels: none -> 145 us  [the longest x1 44.1 us: value_both(): pl.pallas_call(functools.partial(value_kernel, pad, images), grid_spec=pl...]
    all_to_all x0 -> x10, waiting for transfers between devices: none -> 118 us  [the longest x7 76.6 us: exchange_mp(): return lax.all_to_all(parts, 'mp', 0, 0)]
    dot_general x19 -> x0, matrix products: 113 us -> none  [the longest x5 18.8 us: per_device(): jnp.dot(ortho_in, ortho_in.T, precision=HIGHEST)]
    all_gather x2 -> x0, waiting for transfers between devices: 102 us -> none  [the longest x1 59.2 us: per_device(): gathered = lax.all_gather(normed, 'mp', axis=0, tiled=True)]
    psum x5 -> x0, blocking collectives: 99.3 us -> none  [the longest x1 39.5 us: per_device(): lax.psum((grad_spatial, grad_patch, model_part), ('dp', 'mp'))]
    all_to_all x0 -> x10, starting transfers between devices: none -> 40.9 us  [the longest x7 29.1 us: exchange_mp(): return lax.all_to_all(parts, 'mp', 0, 0)]
  transfers between devices with their start and end apart: 11 -> 20, of which waited for: 11 -> 10; matrix products, arithmetic and copies ran while one was open for 9% -> 19% of each run, Pallas kernels for 0% -> 14%
where the time goes in v1:
time: 465 us; the launch traced here: 459 us
  Pallas kernels  145 us (31%)
  waiting for transfers between devices  119 us (26%)
  local copies, waits for them, and re-layouts  92 us (20%)
  other arithmetic  51.4 us (11%)
  starting transfers between devices  42.2 us (9%)
  matrix products  5.77 us (1%)
    all_to_all x7, waiting for transfers between devices, exchange_mp(): return lax.all_to_all(parts, 'mp', 0, 0)  76.6 us
    pallas_call x1, Pallas kernels, value_both(): pl.pallas_call(functools.partial(value_kernel, pad, images), grid_spec=pl...  44.1 us
    all_to_all x3, waiting for transfers between devices, exchange_z(): return lax.all_to_all(parts, 'dp', 0, 0, axis_index_groups=groups)  41.9 us
    pallas_call x2, Pallas kernels, muon(): pl.pallas_call(muon_kernel, out_shape=jax.ShapeDtypeStruct(mine.shape, F3...  38.2 us
    all_to_all x7, starting transfers between devices, exchange_mp(): return lax.all_to_all(parts, 'mp', 0, 0)  29.1 us
    pallas_call x1, Pallas kernels, gate_back(): pl.pallas_call(functools.partial(gate_back_kernel, full), grid_spec=pltpu...  25.2 us
    unnamed x98, local copies, waits for them, and re-layouts  25 us
    pallas_call x1, Pallas kernels, gate_forward(): pl.pallas_call(functools.partial(gate_kernel, chunk), grid=(images,), in_...  23.6 us
  transfers between devices with their start and end apart: 20, of which 10 were waited for; matrix products, arithmetic and copies ran while one was open for 19% of the time, Pallas kernels for 14%

profile of v1, /device:TPU:0, one launch (start us, length us, event | category | flops | bytes accessed | tf_op | source)
XLA Modules:
  0.0 458.6 jit_solution(17912087962305058926)
XLA Ops:
  5.8 5.2 %all-to-all-start = ((bf16[4,256,384]{2,1,0:T(8,128)(2,1)}), bf16[4,256,384]{2,1,0:T(8,128)(2,1)S(1)}, u32[]{:S(2)}, u32[]{:S(2)}) async-start(bf16[4,256,384]{2,1,0:T(8,128)(2,1)} %broadcast_in_dim.18), calls=%async_computation | async-start | bytes 1572864 | tf_op jit(solution)/shard_map/all_to_all | solution.py:476
  12.6 9.2 %all-to-all-done = bf16[4,256,384]{2,1,0:T(8,128)(2,1)S(1)} async-done(((bf16[4,256,384]{2,1,0:T(8,128)(2,1)}), bf16[4,256,384]{2,1,0:T(8,128)(2,1)S(1)}, u32[]{:S(2)}, u32[]{:S(2)}) %all-to-all-start) | async-done | bytes 786464 | tf_op jit(solution)/shard_map/all_to_all | solution.py:476
  23.1 4.4 all-to-all-start.2
  32.7 13.6 %all-to-all-done.2 = bf16[4,256,768]{2,1,0:T(8,128)(2,1)} async-done(((bf16[4,256,768]{2,1,0:T(8,128)(2,1)}), bf16[4,256,768]{2,1,0:T(8,128)(2,1)}, u32[]{:S(2)}, u32[]{:S(2)}) %all-to-all-start.2) | async-done | bytes 1572896 | tf_op jit(solution)/shard_map/all_to_all | solution.py:476
  46.9 3.6 all-to-all-start.1
  54.6 3.8 reshape.228
  78.4 23.6 %gate_forward.1 = (bf16[1248,1536]{1,0:T(8,128)(2,1)}, bf16[1248,1536]{1,0:T(8,128)(2,1)}, bf16[1248,1536]{1,0:T(8,128)(2,1)}, f32[1248,128]{1,0:T(8,128)S(1)}) custom-call(bf16[1248,512]{1,0:T(8,128)(2,1)S(1)} %add_convert_fusion.normed, bf16[512,1536]{1,0:T(8,128)(2,1)S(1)} %copy-done.5, f32[4,1536]{1,0:T(4,128)S(1)} %bitcast.125), custom_call_target="tpu_custom_call" | custom-call | flops 1962934272 | bytes 15335424 | tf_op jit(solution)/shard_map/gate_forward/pallas_call | solution.py:124
  106.8 44.1 %value_both.1 = (bf16[1248,1536]{1,0:T(8,128)(2,1)}, bf16[1248,1536]{1,0:T(8,128)(2,1)}, bf16[1248,1536]{1,0:T(8,128)(2,1)}, f32[256,1536]{1,0:T(8,128)}, bf16[2...) custom-call(s32[1]{0:T(128)} %bitcast.2.core, ...), custom_call_target="tpu_custom_call" | custom-call | flops 11777605632 | bytes 38338560 | tf_op jit(solution)/shard_map/value_both/pallas_call | solution.py:255
  153.7 25.2 %gate_back.1 = (bf16[1248,1536]{1,0:T(8,128)(2,1)}, f32[256,1536]{1,0:T(8,128)S(1)}, bf16[256,1536]{1,0:T(8,128)(2,1)}, f32[8,1536]{1,0:T(8,128)S(1)}) custom-call(s32[1]{0:T(128)} %bitcast.2.core, bf16[512,1280]{1,0:T(8,128)(2,1)S(1)} %copy-done, bf16[1248,1536]{1,0:T(8,128)(2,1)} %get-tuple-element.47.grad_unit, ...), custom_call_target="tpu_custom_call" | custom-call | flops 1962934272 | bytes 19169280 | tf_op jit(solution)/shard_map/gate_back/pallas_call | solution.py:322
  183.3 14.2 %token_back.1 = (bf16[1248,512]{1,0:T(8,128)(2,1)S(1)}, bf16[1248,512]{1,0:T(8,128)(2,1)S(1)}, f32[24,512]{1,0:T(8,128)S(1)}) custom-call(bf16[1248,512]{1,0:T(8,128)(2,1)S(1)} %bitcast.118, bf16[1248,512]{1,0:T(8,128)(2,1)S(1)} %bitcast.121, bf16[1248,1536]{1,0:T(8,128)(2,1)} %get-tuple-element.45.gated, bf16[1248,1536]{1,0:T(8,128)(2,1)} %get-tuple-element.46.low_value, ...), custom_call_target="tpu_custom_call" | custom-call | flops 5888802816 | bytes 15335424 | tf_op jit(solution)/shard_map/token_back/pallas_call | solution.py:378
  208.6 4.5 all-to-all-start.3
  215.5 18.9 %all-to-all-done.3 = bf16[4,256,814]{1,2,0:T(8,128)(2,1)} async-done(((bf16[4,256,814]{1,2,0:T(8,128)(2,1)}), bf16[4,256,814]{1,2,0:T(8,128)(2,1)}, u32[]{:S(2)}, u32[]{:S(2)}) %all-to-all-start.3) | async-done | bytes 1667104 | tf_op jit(solution)/shard_map/all_to_all | solution.py:476
  241.9 6.8 %all-to-all-done.6 = bf16[4,256,384]{2,1,0:T(8,128)(2,1)S(1)} async-done(((bf16[4,256,384]{2,1,0:T(8,128)(2,1)}), bf16[4,256,384]{2,1,0:T(8,128)(2,1)S(1)}, u32[]{:S(2)}, u32[]{:S(2)}) %all-to-all-start.6) | async-done | bytes 786464 | tf_op jit(solution)/shard_map/all_to_all | solution.py:476
  248.8 4.9 %all-to-all-start.4 = ((bf16[4,64,814]{2,1,0:T(8,128)(2,1)}), bf16[4,64,814]{2,1,0:T(8,128)(2,1)S(1)}, u32[]{:S(2)}, u32[]{:S(2)}) async-start(bf16[4,64,814]{2,1,0:T(8,128)(2,1)} %pad_maximum_fusion.6), calls=%async_computation.4 | async-start | bytes 917504 | tf_op jit(solution)/shard_map/all_to_all | solution.py:482
  253.8 12.1 %all-to-all-done.4 = bf16[4,64,814]{2,1,0:T(8,128)(2,1)S(1)} async-done(((bf16[4,64,814]{2,1,0:T(8,128)(2,1)}), bf16[4,64,814]{2,1,0:T(8,128)(2,1)S(1)}, u32[]{:S(2)}, u32[]{:S(2)}) %all-to-all-start.4) | async-done | bytes 416800 | tf_op jit(solution)/shard_map/all_to_all | solution.py:482
  272.6 17.4 %all-to-all-done.7 = bf16[4,256,384]{2,1,0:T(8,128)(2,1)S(1)} async-done(((bf16[4,256,384]{2,1,0:T(8,128)(2,1)}), bf16[4,256,384]{2,1,0:T(8,128)(2,1)S(1)}, u32[]{:S(2)}, u32[]{:S(2)}) %all-to-all-start.7) | async-done | bytes 786464 | tf_op jit(solution)/shard_map/all_to_all | solution.py:482
  294.5 12.3 %all-to-all-done.5 = bf16[4,64,814]{2,1,0:T(8,128)(2,1)S(1)} async-done(((bf16[4,64,814]{2,1,0:T(8,128)(2,1)}), bf16[4,64,814]{2,1,0:T(8,128)(2,1)S(1)}, u32[]{:S(2)}, u32[]{:S(2)}) %all-to-all-start.5) | async-done | bytes 416800 | tf_op jit(solution)/shard_map/all_to_all | solution.py:482
  319.1 4.5 all-to-all-start.8
  324.3 20.6 %all-to-all-done.8 = bf16[4,256,814]{1,2,0:T(8,128)(2,1)} async-done(((bf16[4,256,814]{1,2,0:T(8,128)(2,1)}), bf16[4,256,814]{1,2,0:T(8,128)(2,1)}, u32[]{:S(2)}, u32[]{:S(2)}) %all-to-all-start.8) | async-done | bytes 1667104 | tf_op jit(solution)/shard_map/all_to_all | solution.py:476
  353.8 7.5 %all-to-all-done.9 = bf16[4,256,384]{2,1,0:T(8,128)(2,1)S(1)} async-done(((bf16[4,256,384]{2,1,0:T(8,128)(2,1)}), bf16[4,256,384]{2,1,0:T(8,128)(2,1)S(1)}, u32[]{:S(2)}, u32[]{:S(2)}) %all-to-all-start.9) | async-done | bytes 786464 | tf_op jit(solution)/shard_map/all_to_all | solution.py:476
  381.3 3.8 copy.248
  405.6 17.0 %muon.3 = f32[512,384]{1,0:T(8,128)S(1)} custom-call(bf16[512,1536]{1,0:T(8,128)(2,1)S(1)} %copy.254.moments, f32[512,384]{1,0:T(8,128)S(1)} %get-tuple-element.236.mine), custom_call_target="tpu_custom_call" | custom-call | flops 14495514624 | bytes 6291456 | tf_op jit(solution)/shard_map/muon/pallas_call | solution.py:428
  428.7 21.1 %muon.2 = f32[512,768]{1,0:T(8,128)S(1)} custom-call(bf16[512,3072]{1,0:T(8,128)(2,1)} %maximum_maximum_fusion.moments, f32[512,768]{1,0:T(8,128)S(1)} %copy-done.6), custom_call_target="tpu_custom_call" | custom-call | flops 15300820992 | bytes 12582912 | tf_op jit(solution)/shard_map/muon/pallas_call | solution.py:428
  452.0 3.7 multiply_subtract_fusion
  (263 shorter events, 153.9 us)
Async XLA Ops:
  5.8 16.0 %all-to-all-start = ((bf16[4,256,384]{2,1,0:T(8,128)(2,1)}), bf16[4,256,384]{2,1,0:T(8,128)(2,1)S(1)}, u32[]{:S(2)}, u32[]{:S(2)}) async-start(bf16[4,256,384]{2,1,0:T(8,128)(2,1)} %broadcast_in_dim.18), calls=%async_computation | async-start | bytes 1572864 | tf_op jit(solution)/shard_map/all_to_all | solution.py:476
  23.1 23.1 %all-to-all-start.2 = ((bf16[4,256,768]{2,1,0:T(8,128)(2,1)}), bf16[4,256,768]{2,1,0:T(8,128)(2,1)}, u32[]{:S(2)}, u32[]{:S(2)}) async-start(bf16[4,256,768]{2,1,0:T(8,128)(2,1)} %broadcast_in_dim.20), calls=%async_computation.2 | async-start | bytes 3145728 | tf_op jit(solution)/shard_map/all_to_all | solution.py:476
  32.7 41.6 %collective-permute-start = (bf16[256,1536]{1,0:T(8,128)(2,1)}, bf16[256,1536]{1,0:T(8,128)(2,1)}, u32[]{:S(2)}, u32[]{:S(2)}) collective-permute-start(bf16[256,1536]{1,0:T(8,128)(2,1)} %bitcast.51), channel_id=1, source_target_pairs={{0,4},{4,0},{8,12},{12,8},{16,20},{20,16},{24,28},{28,24},{1,5},{5... | collective-permute-start | bytes 2359304 | tf_op jit(solution)/shard_map/ppermute | solution.py:466
  46.9 30.1 %all-to-all-start.1 = ((f32[4,4,384]{2,1,0:T(4,128)}), f32[4,4,384]{2,1,0:T(4,128)S(1)}, u32[]{:S(2)}, u32[]{:S(2)}) async-start(f32[4,4,384]{2,1,0:T(4,128)} %broadcast_in_dim.19), calls=%async_computation.1 | async-start | bytes 49152 | tf_op jit(solution)/shard_map/all_to_all | solution.py:476
  58.4 43.7 %collective-permute-start.1 = (bf16[256,3072]{1,0:T(8,128)(2,1)}, bf16[256,3072]{1,0:T(8,128)(2,1)}, u32[]{:S(2)}, u32[]{:S(2)}) collective-permute-start(bf16[256,3072]{1,0:T(8,128)(2,1)} %reshape.228), channel_id=1, source_target_pairs={{0,4},{4,0},{8,12},{12,8},{16,20},{20,16},{24,28},{28,24},{1,5},{5... | collective-permute-start | bytes 4718600 | tf_op jit(solution)/shard_map/ppermute | solution.py:466
  58.9 18.1 %copy-start.1 = (bf16[1248,512]{1,0:T(8,128)(2,1)}, bf16[1248,512]{1,0:T(8,128)(2,1)S(1)}, u32[]{:S(2)}) copy-start(bf16[1248,512]{1,0:T(8,128)(2,1)S(1)} %add_convert_fusion.normed) | copy-start | bytes 3833860
  77.0 25.1 %copy-start.10 = (f32[4,4,384]{2,1,0:T(4,128)}, f32[4,4,384]{2,1,0:T(4,128)S(1)}, u32[]{:S(2)}) copy-start(f32[4,4,384]{2,1,0:T(4,128)S(1)} %all-to-all-done.1) | copy-start | bytes 73732
  106.8 44.7 %copy-start = (bf16[512,1280]{1,0:T(8,128)(2,1)S(1)}, bf16[512,1280]{1,0:T(8,128)(2,1)}, u32[]{:S(2)}) copy-start(bf16[512,1280]{1,0:T(8,128)(2,1)} %pad.24.clone.normed_t) | copy-start | bytes 3932164
  150.9 50.2 %collective-permute-start.2 = (bf16[256,1536]{1,0:T(8,128)(2,1)}, bf16[256,1536]{1,0:T(8,128)(2,1)}, u32[]{:S(2)}, u32[]{:S(2)}) collective-permute-start(bf16[256,1536]{1,0:T(8,128)(2,1)} %get-tuple-element.56), channel_id=1, source_target_pairs={{0,4},{4,0},{8,12},{12,8},{16,20},{20,16},{24,28},{28,24},{1,5},{5... | collective-permute-start | bytes 2359304 | tf_op jit(solution)/shard_map/ppermute | solution.py:466
  199.6 1.4 collective-permute-start.4
  199.7 3.6 collective-permute-start.3
  200.1 13.0 %collective-permute-start.6 = (bf16[256,1536]{1,0:T(8,128)(2,1)}, bf16[256,1536]{1,0:T(8,128)(2,1)}, u32[]{:S(2)}, u32[]{:S(2)}) collective-permute-start(bf16[256,1536]{1,0:T(8,128)(2,1)} %get-tuple-element.65), channel_id=1, source_target_pairs={{0,4},{4,0},{8,12},{12,8},{16,20},{20,16},{24,28},{28,24},{1,5},{5... | collective-permute-start | bytes 2359304 | tf_op jit(solution)/shard_map/ppermute | solution.py:466
  208.6 25.7 %all-to-all-start.3 = ((bf16[4,256,814]{1,2,0:T(8,128)(2,1)}), bf16[4,256,814]{1,2,0:T(8,128)(2,1)}, u32[]{:S(2)}, u32[]{:S(2)}) async-start(bf16[4,256,814]{1,2,0:T(8,128)(2,1)} %pad_maximum_fusion), calls=%async_computation.3 | async-start | bytes 3342336 | tf_op jit(solution)/shard_map/all_to_all | solution.py:476
  234.4 14.4 %all-to-all-start.6 = ((bf16[4,256,384]{2,1,0:T(8,128)(2,1)}), bf16[4,256,384]{2,1,0:T(8,128)(2,1)S(1)}, u32[]{:S(2)}, u32[]{:S(2)}) async-start(bf16[4,256,384]{2,1,0:T(8,128)(2,1)} %bitcast.115), calls=%async_computation.6 | async-start | bytes 1572864 | tf_op jit(solution)/shard_map/all_to_all | solution.py:476
  248.8 17.2 %all-to-all-start.4 = ((bf16[4,64,814]{2,1,0:T(8,128)(2,1)}), bf16[4,64,814]{2,1,0:T(8,128)(2,1)S(1)}, u32[]{:S(2)}, u32[]{:S(2)}) async-start(bf16[4,64,814]{2,1,0:T(8,128)(2,1)} %pad_maximum_fusion.6), calls=%async_computation.4 | async-start | bytes 917504 | tf_op jit(solution)/shard_map/all_to_all | solution.py:482
  267.0 23.1 %all-to-all-start.7 = ((bf16[4,256,384]{2,1,0:T(8,128)(2,1)}), bf16[4,256,384]{2,1,0:T(8,128)(2,1)S(1)}, u32[]{:S(2)}, u32[]{:S(2)}) async-start(bf16[4,256,384]{2,1,0:T(8,128)(2,1)} %broadcast_in_dim.24), calls=%async_computation.7 | async-start | bytes 1572864 | tf_op jit(solution)/shard_map/all_to_all | solution.py:482
  290.8 16.0 %all-to-all-start.5 = ((bf16[4,64,814]{2,1,0:T(8,128)(2,1)}), bf16[4,64,814]{2,1,0:T(8,128)(2,1)S(1)}, u32[]{:S(2)}, u32[]{:S(2)}) async-start(bf16[4,64,814]{2,1,0:T(8,128)(2,1)} %broadcast_in_dim.23), calls=%async_computation.5 | async-start | bytes 917504 | tf_op jit(solution)/shard_map/all_to_all | solution.py:482
  294.4 14.8 %collective-permute-start.7 = (f32[256,384]{1,0:T(8,128)S(1)}, f32[256,384]{1,0:T(8,128)}, u32[]{:S(2)}, u32[]{:S(2)}) collective-permute-start(f32[256,384]{1,0:T(8,128)S(1)} %convert_reduce_fusion.1), channel_id=1, source_target_pairs={{0,4},{4,0},{8,12},{12,8},{16,20},{20,16},{24,28},{28,24},{1,5},{5... | collective-permute-start | bytes 1179656 | tf_op jit(solution)/shard_map/ppermute | solution.py:466
  307.9 3.5 collective-permute-start.5
  319.1 25.8 %all-to-all-start.8 = ((bf16[4,256,814]{1,2,0:T(8,128)(2,1)}), bf16[4,256,814]{1,2,0:T(8,128)(2,1)}, u32[]{:S(2)}, u32[]{:S(2)}) async-start(bf16[4,256,814]{1,2,0:T(8,128)(2,1)} %broadcast_in_dim.25), calls=%async_computation.8 | async-start | bytes 3342336 | tf_op jit(solution)/shard_map/all_to_all | solution.py:476
  346.8 14.5 %all-to-all-start.9 = ((bf16[4,256,384]{2,1,0:T(8,128)(2,1)}), bf16[4,256,384]{2,1,0:T(8,128)(2,1)S(1)}, u32[]{:S(2)}, u32[]{:S(2)}) async-start(bf16[4,256,384]{2,1,0:T(8,128)(2,1)} %broadcast_in_dim.26), calls=%async_computation.9 | async-start | bytes 1572864 | tf_op jit(solution)/shard_map/all_to_all | solution.py:476
  353.8 36.3 %collective-permute-start.8 = (bf16[256,4,814]{0,1,2:T(4,128)(2,1)}, bf16[256,4,814]{0,1,2:T(4,128)(2,1)}, u32[]{:S(2)}, u32[]{:S(2)}) collective-permute-start(bf16[256,4,814]{0,1,2:T(4,128)(2,1)} %copy.235), channel_id=1, source_target_pairs={{0,4},{4,0},{8,12},{12,8},{16,20},{20,16},{24,28},{28,24},{1,5},{5... | collective-permute-start | bytes 5001224 | tf_op jit(solution)/shard_map/ppermute | solution.py:466
  362.3 25.2 %collective-permute-start.9 = (bf16[256,1536]{1,0:T(8,128)(2,1)}, bf16[256,1536]{1,0:T(8,128)(2,1)}, u32[]{:S(2)}, u32[]{:S(2)}) collective-permute-start(bf16[256,1536]{1,0:T(8,128)(2,1)} %bitcast.53), channel_id=1, source_target_pairs={{0,4},{4,0},{8,12},{12,8},{16,20},{20,16},{24,28},{28,24},{1,5},{5... | collective-permute-start | bytes 2359304 | tf_op jit(solution)/shard_map/ppermute | solution.py:466
  405.6 17.1 %copy-start.24 = (f32[384,512]{0,1:T(8,128)S(1)}, f32[384,512]{0,1:T(8,128)}, u32[]{:S(2)}) copy-start(f32[384,512]{0,1:T(8,128)} %copy.245) | copy-start | bytes 2359300
  (39 other events, 141.6 us)
